TPU v7x, 32 devices: a whole 2x2x4 slice. The times are simulated.
32 devices in a mesh: groups: 2 (over y), choice: 4 (over z), fsdp: 4 (over x, core).
Axes of the slice: x: 2, y: 2, z: 4, core: 2. Of those that a mesh axis runs over, the one named last changes fastest.
Arguments:
- hidden: bfloat16 [2048, 4096], P(('groups', 'choice'), 'fsdp'), parts along dimension 0, may hold values from -6 to 6
- norm_gain: float32 [4096], replicated, may hold values from 0.25 to 1.75
- query_weight: bfloat16 [4096, 4096], P('choice', 'fsdp'), may hold values from -0.09375 to 0.09375
- out_weight: bfloat16 [4096, 4096], P('fsdp', 'choice'), may hold values from -0.09375 to 0.09375
- enc_keys: bfloat16 [8, 256, 4096], P(('groups', 'choice'), None, 'fsdp'), parts along dimension 0, may hold values from -480 to 480
- enc_values: bfloat16 [8, 256, 4096], P(('groups', 'choice'), None, 'fsdp'), parts along dimension 0, may hold values from -24 to 24
- slot_question: int32 [32], P(('groups', 'choice')), parts along dimension 0, may hold values from 0 to 3, as said below
- answer_len: int32 [32], P(('groups', 'choice')), parts along dimension 0, may hold values from 16 to 64
Outputs:
- output: bfloat16 [2048, 4096], P(('groups', 'choice', 'fsdp')), parts along dimension 0
There are 2 independent parts, one for each index of `groups`. A program takes and returns all parts, laid end to end along the dimension named above; an argument that names none is the same for every part. Nothing has to cross between parts.
Inputs may be any that keep to these rules, and one draw needn't show every extreme that they name: `slot_question`: every question is named by two or more answer choices; the 4 answer choices of one device name no question more than 2 times, and every device names some question exactly 2 times.
All inputs are finite; a program needn't handle non-finite values.
Results may differ from a plain program's by a relative error of at most 0.017.
Values may be sent and summed in bfloat16 or wider, within the bound.
A program may use at most 64 MiB of HBM per device.

v0:
```python
import math

import jax
import jax.numpy as jnp
from jax import lax
from jax.sharding import PartitionSpec as P

HD = 64
CAP = 2


epsilon = 1e-06


def attend_rows(query_rows, keys_block, values_block):
    count = query_rows.shape[0]
    width = query_rows.shape[1]
    heads_here = width // HD
    scale = 1.0 / math.sqrt(HD)
    query_view = query_rows.reshape(count, heads_here, HD)
    key_view = keys_block.reshape(keys_block.shape[0], heads_here, HD)
    value_view = values_block.reshape(values_block.shape[0], heads_here, HD)
    scores = (
        jnp.einsum("ahd,khd->hak", query_view, key_view, preferred_element_type=jnp.float32) * scale
    )
    weights = jax.nn.softmax(scores, axis=-1).astype(jnp.bfloat16)
    context = jnp.einsum("hak,khd->ahd", weights, value_view, preferred_element_type=jnp.float32)
    return context.astype(jnp.bfloat16).reshape(count, width)


def on_device(
    hidden, norm_gain, query_weight, out_weight, enc_keys, enc_values, slot_question, answer_len
):
    whole = lax.all_gather(hidden, "fsdp", axis=1, tiled=True)
    widened = whole.astype(jnp.float32)
    total_rows = widened.shape[0]
    slots_here = slot_question.shape[0]
    answer_rows = total_rows // slots_here
    inverse = lax.rsqrt(jnp.mean(widened * widened, axis=-1, keepdims=True) + epsilon)
    normed = (widened * inverse * norm_gain).astype(jnp.bfloat16)
    columns = query_weight.shape[1]
    section = normed
    queries = jnp.dot(
        section,
        lax.all_gather(query_weight, "choice", axis=0, tiled=True),
        preferred_element_type=jnp.float32,
    ).astype(jnp.bfloat16)
    per_slot = queries.reshape(slots_here, answer_rows, columns)
    owners = lax.axis_size("choice")
    buffers = owners * CAP
    slot_ids = jnp.arange(slots_here, dtype=jnp.int32)
    earlier = slot_ids[:, None] > slot_ids[None, :]
    same_question = slot_question[:, None] == slot_question[None, :]
    rank = jnp.sum(jnp.where(same_question & earlier, 1, 0), axis=1).astype(jnp.int32)
    target = slot_question * CAP + rank
    placed = jnp.arange(buffers, dtype=jnp.int32)[:, None] == target[None, :]
    source_slot = jnp.sum(jnp.where(placed, slot_ids[None, :], 0), axis=1)
    filled = jnp.any(placed, axis=1)
    outgoing = jnp.where(filled[:, None, None], per_slot[source_slot], jnp.zeros((), jnp.bfloat16))
    outgoing = outgoing.reshape(owners, CAP, answer_rows, columns)
    local_keys = enc_keys[0]
    local_values = enc_values[0]

    def answer_source(block):
        flat_rows = block.reshape(-1, columns)
        return attend_rows(flat_rows, local_keys, local_values).reshape(block.shape)

    answered = lax.map(
        answer_source, lax.all_to_all(outgoing, "choice", split_axis=0, concat_axis=0, tiled=True)
    )
    returned = lax.all_to_all(answered, "choice", split_axis=0, concat_axis=0, tiled=True)
    context = returned.reshape(buffers, answer_rows, columns)[target]
    context_rows = context.reshape(total_rows, columns)
    out_full = lax.all_gather(out_weight, "choice", axis=1, tiled=True)
    share = total_rows // lax.axis_size("fsdp")
    section = context_rows
    mixed = lax.psum_scatter(
        jnp.dot(section, out_full, preferred_element_type=jnp.float32).astype(jnp.bfloat16),
        "fsdp",
        scatter_dimension=0,
        tiled=True,
    ).astype(jnp.float32)
    offset = lax.axis_index("fsdp") * share
    residual = lax.dynamic_slice_in_dim(widened, offset, share, 0)
    positions = offset + jnp.arange(share, dtype=jnp.int32)
    slot_index = positions // answer_rows
    matching = slot_index[:, None] == jnp.arange(slots_here, dtype=jnp.int32)[None, :]
    lengths = jnp.sum(jnp.where(matching, answer_len[None, :], 0), axis=1)
    valid = positions % answer_rows < lengths
    return jnp.where(valid[:, None], residual + mixed, 0.0).astype(jnp.bfloat16)


def solution(mesh):
    in_specs = (
        P(("groups", "choice"), "fsdp"),
        P(),
        P("choice", "fsdp"),
        P("fsdp", "choice"),
        P(("groups", "choice"), None, "fsdp"),
        P(("groups", "choice"), None, "fsdp"),
        P(("groups", "choice")),
        P(("groups", "choice")),
    )
    out_specs = P(("groups", "choice", "fsdp"), None)
    return jax.shard_map(
        on_device, mesh=mesh, in_specs=in_specs, out_specs=out_specs, check_vma=False
    )
```

profile of v0, /device:TPU:15, one launch (start us, length us, event | category | flops | bytes accessed | tf_op | source)
XLA Modules:
  0.0 423.0 jit_solution(3458206566313379897)
XLA Ops:
  6.5 0.7 all-gather.4.cloned.1.call-update
  7.3 0.7 all-gather.6.cloned.1.call-update
  8.1 0.7 all-gather.8.cloned.1.call-update
  9.2 22.9 %all-gather.4.cloned.1.call-done = bf16[256,4096]{1,0:T(8,128)(2,1)} async-done(((bf16[256,1024]{1,0:T(8,128)(2,1)}), bf16[256,4096]{1,0:T(8,128)(2,1)}) %all-gather.4.cloned.1.call-update) | async-done | bytes 2097168 | tf_op jit(solution)/shard_map/all_gather | solution.py:34
  32.1 2.2 multiply_reduce_fusion.1
  34.4 146.8 %all-gather.6.cloned.1.call-done = bf16[4096,1024]{1,0:T(8,128)(2,1)} async-done(((bf16[1024,1024]{1,0:T(8,128)(2,1)}), bf16[4096,1024]{1,0:T(8,128)(2,1)}) %all-gather.6.cloned.1.call-update) | async-done | bytes 8388624 | tf_op jit(solution)/shard_map/all_gather | solution.py:45
  181.1 6.6 %fusion.28 = bf16[256,1024]{1,0:T(8,128)(2,1)} fusion(bf16[4096,1024]{1,0:T(8,128)(2,1)} %all-gather.6.cloned.1.call-done, f32[4096]{0:T(1024)S(1)} %copy-done.5, f32[256]{0:T(256)S(1)} %add_rsqrt_fusion, bf16[256,4096]{1,0:T(8,128)(2,1)S(1)} %copy-done), kind=kOutput, calls=%fused_computation.24 | convolution fusion | flops 2151940096 | bytes 11027456 | tf_op jit(solution)/shard_map/dot_general | solution.py:43
  187.7 1.7 gather_fusion
  189.3 1.1 broadcast_select_fusion
  190.5 7.7 %all-to-all-start = ((bf16[4,2,64,1024]{3,2,1,0:T(8,128)(2,1)}), bf16[4,2,64,1024]{3,2,1,0:T(8,128)(2,1)}, u32[]{:S(2)}, u32[]{:S(2)}) async-start(bf16[4,2,64,1024]{3,2,1,0:T(8,128)(2,1)} %broadcast_select_fusion), calls=%async_computation | async-start | bytes 2097152 | tf_op jit(solution)/shard_map/all_to_all | solution.py:69
  198.1 1.0 copy.17
  199.1 1.0 copy.18
  200.1 44.6 %all-to-all-done = bf16[4,2,64,1024]{3,2,1,0:T(8,128)(2,1)} async-done(((bf16[4,2,64,1024]{3,2,1,0:T(8,128)(2,1)}), bf16[4,2,64,1024]{3,2,1,0:T(8,128)(2,1)}, u32[]{:S(2)}, u32[]{:S(2)}) %all-to-all-start) | async-done | bytes 1048608 | tf_op jit(solution)/shard_map/all_to_all | solution.py:69
  244.8 38.1 %while.11 = (s32[]{:T(128)}, bf16[4,2,64,1024]{3,2,1,0:T(8,128)(2,1)}, bf16[4,2,64,1024]{3,2,1,0:T(8,128)(2,1)}, bf16[1,256,1024]{1,2,0:T(8,128)(2,1)}, bf16[1,256,1024]{1,2,0:T(8,128)(2,1)}) while((s32[]{:T(128)}, bf16[4,2,64,1024]{3,2,1,0:T(8,128)(2,1)}, bf16[4,2,64,1024]{3,2,1,0:T(8,128)(2,1)}, bf16[1,256,1024]{1,2,0:T(8,128)(2,1)}, ...), condition=%wide.region_8.9_spmd.clone, body=%wide.region_5.8_spmd.sunk.clone | while | flops 205130240 | bytes 7094377 | solution.py:68
  244.8 1.0 constant_dynamic-slice_fusion.3
  245.8 0.3 reshape.108
  246.1 2.0 fusion.64
  248.2 4.8 %fusion.65 = bf16[128,16,64]{0,2,1:T(8,128)(2,1)S(1)} fusion(bf16[256,16,64]{0,2,1:T(8,128)(2,1)} %bitcast.38, f32[16,128]{1,0:T(8,128)S(1)} %fusion.64, bf16[256,16,64]{0,2,1:T(8,128)(2,1)S(1)} %bitcast.44, bf16[128,16,64]{2,1,0:T(8,128)(2,1)S(1)} %reshape.108), kind=kOutput, calls=%fused_computation.8.clone.1.clone | convolution fusion | flops 136448256 | bytes 1581056 | tf_op jit(solution)/shard_map/while/body/eval_jaxpr/hak,khd->ahd/dot_general | solution.py:27
  252.9 0.2 reshape.109
  253.2 0.4 copy.42
  253.6 0.7 constant_dynamic-update-slice_fusion.3
  254.3 1.0 constant_dynamic-slice_fusion.3
  255.3 0.3 reshape.108
  255.6 2.0 fusion.64
  257.7 4.8 %fusion.65 = bf16[128,16,64]{0,2,1:T(8,128)(2,1)S(1)} fusion(bf16[256,16,64]{0,2,1:T(8,128)(2,1)} %bitcast.38, f32[16,128]{1,0:T(8,128)S(1)} %fusion.64, bf16[256,16,64]{0,2,1:T(8,128)(2,1)S(1)} %bitcast.44, bf16[128,16,64]{2,1,0:T(8,128)(2,1)S(1)} %reshape.108), kind=kOutput, calls=%fused_computation.8.clone.1.clone | convolution fusion | flops 136448256 | bytes 1581056 | tf_op jit(solution)/shard_map/while/body/eval_jaxpr/hak,khd->ahd/dot_general | solution.py:27
  262.7 0.4 copy.42
  263.1 0.7 constant_dynamic-update-slice_fusion.3
  263.8 1.0 constant_dynamic-slice_fusion.3
  264.8 0.3 reshape.108
  265.2 2.0 fusion.64
  267.2 4.8 %fusion.65 = bf16[128,16,64]{0,2,1:T(8,128)(2,1)S(1)} fusion(bf16[256,16,64]{0,2,1:T(8,128)(2,1)} %bitcast.38, f32[16,128]{1,0:T(8,128)S(1)} %fusion.64, bf16[256,16,64]{0,2,1:T(8,128)(2,1)S(1)} %bitcast.44, bf16[128,16,64]{2,1,0:T(8,128)(2,1)S(1)} %reshape.108), kind=kOutput, calls=%fused_computation.8.clone.1.clone | convolution fusion | flops 136448256 | bytes 1581056 | tf_op jit(solution)/shard_map/while/body/eval_jaxpr/hak,khd->ahd/dot_general | solution.py:27
  272.2 0.4 copy.42
  272.6 0.7 constant_dynamic-update-slice_fusion.3
  273.4 1.0 constant_dynamic-slice_fusion.3
  274.4 0.3 reshape.108
  274.7 2.0 fusion.64
  276.7 4.8 %fusion.65 = bf16[128,16,64]{0,2,1:T(8,128)(2,1)S(1)} fusion(bf16[256,16,64]{0,2,1:T(8,128)(2,1)} %bitcast.38, f32[16,128]{1,0:T(8,128)S(1)} %fusion.64, bf16[256,16,64]{0,2,1:T(8,128)(2,1)S(1)} %bitcast.44, bf16[128,16,64]{2,1,0:T(8,128)(2,1)S(1)} %reshape.108), kind=kOutput, calls=%fused_computation.8.clone.1.clone | convolution fusion | flops 136448256 | bytes 1581056 | tf_op jit(solution)/shard_map/while/body/eval_jaxpr/hak,khd->ahd/dot_general | solution.py:27
  281.8 0.4 copy.42
  282.2 0.7 constant_dynamic-update-slice_fusion.3
  282.9 7.9 %all-to-all-start.1 = ((bf16[4,2,64,1024]{3,2,1,0:T(8,128)(2,1)}), bf16[4,2,64,1024]{3,2,1,0:T(8,128)(2,1)S(1)}, u32[]{:S(2)}, u32[]{:S(2)}) async-start(bf16[4,2,64,1024]{3,2,1,0:T(8,128)(2,1)} %get-tuple-element.32), calls=%async_computation.1 | async-start | bytes 2097152 | tf_op jit(solution)/shard_map/all_to_all | solution.py:71
  290.8 49.3 %all-to-all-done.1 = bf16[4,2,64,1024]{3,2,1,0:T(8,128)(2,1)S(1)} async-done(((bf16[4,2,64,1024]{3,2,1,0:T(8,128)(2,1)}), bf16[4,2,64,1024]{3,2,1,0:T(8,128)(2,1)S(1)}, u32[]{:S(2)}, u32[]{:S(2)}) %all-to-all-start.1) | async-done | bytes 1048608 | tf_op jit(solution)/shard_map/all_to_all | solution.py:71
  340.1 1.4 gather_fusion.1
  341.5 32.7 %all-gather.8.cloned.1.call-done = bf16[1024,4096]{1,0:T(8,128)(2,1)} async-done(((bf16[1024,1024]{1,0:T(8,128)(2,1)}), bf16[1024,4096]{1,0:T(8,128)(2,1)}) %all-gather.8.cloned.1.call-update) | async-done | bytes 8388624 | tf_op jit(solution)/shard_map/all_gather | solution.py:74
  374.2 7.3 %convolution_convert_fusion.1 = bf16[256,4096]{1,0:T(8,128)(2,1)} fusion(bf16[256,1024]{1,0:T(8,128)(2,1)} %bitcast.45, bf16[1024,4096]{1,0:T(8,128)(2,1)} %all-gather.8.cloned.1.call-done), kind=kOutput, calls=%fused_computation.17 | convolution fusion | flops 2148532224 | bytes 11010048 | tf_op jit(solution)/shard_map/dot_general | solution.py:78
  381.6 0.6 copy-done.6
  382.3 2.4 convert_element_type.27
  384.7 29.4 %reduce-scatter.2.cloned.1.call-done = bf16[64,4096]{1,0:T(8,128)(2,1)} async-done(((bf16[256,4096]{1,0:T(8,128)(2,1)}), bf16[64,4096]{1,0:T(8,128)(2,1)}) %reduce-scatter.2.cloned.1.call-update) | async-done | bytes 524304 | tf_op jit(solution)/shard_map/reduce_scatter | solution.py:77
  414.1 2.3 select_convert_fusion
  (40 shorter events, 1.5 us)
Async XLA Ops:
  6.5 25.6 %all-gather.4.cloned.1.call-start = ((), (), s32[]{:S(2)}) async-start(), calls=%async_computation.3 | async-start | bytes 2621440 | tf_op jit(solution)/shard_map/all_gather | solution.py:34
  7.3 1.5 copy-start.4
  7.3 173.9 %all-gather.6.cloned.1.call-start = ((), (), s32[]{:S(2)}) async-start(), calls=%async_computation.4 | async-start | bytes 10485760 | tf_op jit(solution)/shard_map/all_gather | solution.py:45
  8.0 173.1 %copy-start.5 = (f32[4096]{0:T(1024)S(1)}, f32[4096]{0:T(1024)}, u32[]{:S(2)}) copy-start(f32[4096]{0:T(1024)} %param.11) | copy-start | bytes 49156
  8.0 366.2 %all-gather.8.cloned.1.call-start = ((), (), s32[]{:S(2)}) async-start(), calls=%async_computation.5 | async-start | bytes 10485760 | tf_op jit(solution)/shard_map/all_gather | solution.py:74
  32.1 149.0 %copy-start = (bf16[256,4096]{1,0:T(8,128)(2,1)S(1)}, bf16[256,4096]{1,0:T(8,128)(2,1)}, u32[]{:S(2)}) copy-start(bf16[256,4096]{1,0:T(8,128)(2,1)} %all-gather.4.cloned.1.call-done) | copy-start | bytes 6291460
  190.5 7.7 %copy-start.1 = (bf16[1,256,1024]{2,1,0:T(8,128)(2,1)S(1)}, bf16[1,256,1024]{2,1,0:T(8,128)(2,1)}, u32[]{:S(2)}) copy-start(bf16[1,256,1024]{2,1,0:T(8,128)(2,1)} %param.14) | copy-start | bytes 1572868
  190.5 8.7 %copy-start.2 = (bf16[1,256,1024]{2,1,0:T(8,128)(2,1)S(1)}, bf16[1,256,1024]{2,1,0:T(8,128)(2,1)}, u32[]{:S(2)}) copy-start(bf16[1,256,1024]{2,1,0:T(8,128)(2,1)} %param.15) | copy-start | bytes 1572868
  190.5 54.3 %all-to-all-start = ((bf16[4,2,64,1024]{3,2,1,0:T(8,128)(2,1)}), bf16[4,2,64,1024]{3,2,1,0:T(8,128)(2,1)}, u32[]{:S(2)}, u32[]{:S(2)}) async-start(bf16[4,2,64,1024]{3,2,1,0:T(8,128)(2,1)} %broadcast_select_fusion), calls=%async_computation | async-start | bytes 2097152 | tf_op jit(solution)/shard_map/all_to_all | solution.py:69
  245.7 2.4 copy-start.3
  255.3 2.4 copy-start.3
  264.8 2.4 copy-start.3
  274.3 2.4 copy-start.3
  282.9 57.2 %all-to-all-start.1 = ((bf16[4,2,64,1024]{3,2,1,0:T(8,128)(2,1)}), bf16[4,2,64,1024]{3,2,1,0:T(8,128)(2,1)S(1)}, u32[]{:S(2)}, u32[]{:S(2)}) async-start(bf16[4,2,64,1024]{3,2,1,0:T(8,128)(2,1)} %get-tuple-element.32), calls=%async_computation.1 | async-start | bytes 2097152 | tf_op jit(solution)/shard_map/all_to_all | solution.py:71
  290.8 123.3 %reduce-scatter.2.cloned.1.call-start = ((), (), s32[]{:S(2)}) async-start(), calls=%async_computation.6 | async-start | bytes 2621440 | tf_op jit(solution)/shard_map/reduce_scatter | solution.py:77
  381.5 0.7 copy-start.6
Sparse Core Ops, SparseCore 0:
  8.9 23.1 all-gather.3
  33.7 147.3 all-gather.5
  182.7 191.4 all-gather.7
  381.7 32.4 reduce-scatter.1
where the time goes:
time: 426 us; the launch traced here: 423 us
  waiting for transfers between devices  328 us (77%)
  matrix products  41 us (10%)
  local copies, waits for them, and re-layouts  16.5 us (4%)
  starting transfers between devices  15.7 us (4%)
  between operations  13.2 us (3%)
  other arithmetic  8.61 us (2%)
    all_gather x1, waiting for transfers between devices, on_device(): lax.all_gather(query_weight, 'choice', axis=0, tiled=True)  147 us
    all_to_all x1, waiting for transfers between devices, on_device(): lax.all_to_all(answered, 'choice', split_axis=0, concat_axis=0, tiled=True)  49.3 us
    all_to_all x1, waiting for transfers between devices, on_device(): lax.all_to_all(outgoing, 'choice', split_axis=0, concat_axis=0, tiled=True)  44.6 us
    all_gather x1, waiting for transfers between devices, on_device(): out_full = lax.all_gather(out_weight, 'choice', axis=1, tiled=True)  32.7 us
    reduce_scatter x1, waiting for transfers between devices, on_device(): lax.psum_scatter(jnp.dot(section, out_full, preferred_element_type=jnp.fl...  29.4 us
    all_gather x1, waiting for transfers between devices, on_device(): whole = lax.all_gather(hidden, 'fsdp', axis=1, tiled=True)  22.9 us
    dot_general x4, matrix products, attend_rows(): jnp.einsum('hak,khd->ahd', weights, value_view, preferred_element_type=jn...  19 us
  transfers between devices with their start and end apart: 6, of which 6 were waited for; matrix products, arithmetic and copies ran while one was open for 13% of the time, Pallas kernels for 0%

commit v1 on v0

--- a/solution.py
+++ b/solution.py
@@ -1,8 +1,11 @@
+import functools
 import math
 
 import jax
 import jax.numpy as jnp
 from jax import lax
+from jax.experimental import pallas as pl
+from jax.experimental.pallas import tpu as pltpu
 from jax.sharding import PartitionSpec as P
 
 HD = 64
@@ -10,6 +13,349 @@
 
 
 epsilon = 1e-06
+
+
+def flip(index, bits):
+    result = index
+    bit = 1
+    while bit <= bits:
+        if bits & bit:
+            result = result + bit * (1 - 2 * ((index // bit) % 2))
+        bit *= 2
+    return result
+
+
+def remote(src, dst, send_sem, recv_sem, axis, target):
+    return pltpu.make_async_remote_copy(
+        src_ref=src,
+        dst_ref=dst,
+        send_sem=send_sem,
+        recv_sem=recv_sem,
+        device_id={axis: target},
+        device_id_type=pl.DeviceIdType.MESH,
+    )
+
+
+def block_kernel(
+    C,
+    F,
+    answer_rows,
+    hidden,
+    gain,
+    wq,
+    wo,
+    keys,
+    values,
+    questions,
+    lengths,
+    out,
+    hrow,
+    xs,
+    xn,
+    qs,
+    qr,
+    kb,
+    vb,
+    sq,
+    sq_s,
+    ctx,
+    osend,
+    orecv,
+    asend,
+    arecv,
+    a_s,
+    a_r,
+    b_s,
+    b_r,
+    c_s,
+    c_r,
+    kv_s,
+    kv_r,
+    sq_ss,
+    sq_r,
+    d_s,
+    d_r,
+    e_s,
+    e_r,
+    g_s,
+    g_r,
+    h_s,
+    h_r,
+    local,
+):
+    c = lax.axis_index("choice")
+    f = lax.axis_index("fsdp")
+    rq = hidden.shape[0] // F
+    df = hidden.shape[1]
+    D = df * F
+    kc = wq.shape[0]
+    hc = wq.shape[1] // C
+    rows = C * rq
+    heads = hc // HD
+    scale = 1.0 / math.sqrt(HD)
+
+    choice_peers = [(lax.rem(c + t, C)) for t in range(1, C)]
+    fsdp_peers = [flip(f, k) for k in range(1, F)]
+
+    barrier = pltpu.get_barrier_semaphore()
+    for p in choice_peers:
+        pl.semaphore_signal(barrier, inc=1, device_id={"choice": p}, device_id_type=pl.DeviceIdType.MESH)
+    for p in fsdp_peers:
+        pl.semaphore_signal(barrier, inc=1, device_id={"fsdp": p}, device_id_type=pl.DeviceIdType.MESH)
+    pl.semaphore_wait(barrier, C + F - 2)
+
+    pending = []
+
+    def send(*args):
+        copy = remote(*args)
+        copy.start()
+        pending.append(copy)
+
+    def arrived(dst, sem, axis):
+        peer = choice_peers[0] if axis == "choice" else fsdp_peers[0]
+        remote(dst, dst, sem, sem, axis, peer).wait_recv()
+
+    def cols(index, width):
+        return pl.ds(pl.multiple_of(index * width, width), width)
+
+    def part(index):
+        return pl.ds(pl.multiple_of(index * rq, rq), rq)
+
+    for p in fsdp_peers:
+        send(hidden.at[part(p)], hrow.at[:, cols(f, df)], a_s.at[p], a_r.at[f], "fsdp", p)
+    hrow[:, cols(f, df)] = hidden[part(f), :]
+    for p in fsdp_peers:
+        arrived(hrow.at[:, cols(p, df)], a_r.at[p], "fsdp")
+
+    total = jnp.zeros((rq, 1), jnp.float32)
+    for i in range(F):
+        x = hrow[:, i * df : (i + 1) * df].astype(jnp.float32)
+        total = total + jnp.sum(x * x, axis=-1, keepdims=True)
+    inverse = lax.rsqrt(total / D + epsilon)
+
+    def norm_block(i):
+        x = hrow[:, cols(i, kc)].astype(jnp.float32)
+        return (x * inverse * gain[:, cols(i, kc)]).astype(jnp.bfloat16)
+
+    for p in choice_peers:
+        xs[p] = norm_block(p)
+        send(xs.at[p], xn.at[f, c], b_s.at[p], b_r.at[c], "choice", p)
+    xn[f, c] = norm_block(c)
+
+    for p in fsdp_peers:
+        send(xn.at[f, c], xn.at[f, c], c_s.at[p, c], c_r.at[f, c], "fsdp", p)
+    for p in choice_peers:
+        send(questions, sq.at[c], sq_ss.at[p], sq_r.at[c], "choice", p)
+    for p in choice_peers:
+        arrived(xn.at[f, p], b_r.at[p], "choice")
+        for o in fsdp_peers:
+            send(xn.at[f, p], xn.at[f, p], c_s.at[o, p], c_r.at[f, p], "fsdp", o)
+
+    for p in choice_peers:
+        send(keys.at[:, cols(p, hc)], kb.at[c], kv_s.at[0, p], kv_r.at[0, c], "choice", p)
+        send(values.at[:, cols(p, hc)], vb.at[c], kv_s.at[1, p], kv_r.at[1, c], "choice", p)
+    kb[c] = keys[:, cols(c, hc)]
+    vb[c] = values[:, cols(c, hc)]
+    sq[c] = questions[...]
+
+    head_of_lane = lax.broadcasted_iota(jnp.int32, (1, hc), 1) // HD
+
+    def project(k):
+        j = flip(f, k)
+        if k > 0:
+            for i in range(C):
+                arrived(xn.at[j, i], c_r.at[j, i], "fsdp")
+        for t in range(1, C + 1):
+            p = lax.rem(c + t, C)
+            acc = jnp.dot(
+                xn[j].reshape(rows, kc), wq[:, cols(p, hc)], preferred_element_type=jnp.float32
+            ).astype(jnp.bfloat16)
+            if t < C:
+                qs[j, p] = acc
+                send(qs.at[j, p], qr.at[j, c], d_s.at[j, p], d_r.at[j, c], "choice", p)
+            else:
+                qr[j, c] = acc
+
+    def attend(k):
+        j = flip(f, k)
+        if k == 0:
+            for p in choice_peers:
+                arrived(sq.at[p], sq_r.at[p], "choice")
+            copy = pltpu.make_async_copy(sq, sq_s, local)
+            copy.start()
+            copy.wait()
+        for p in choice_peers:
+            arrived(qr.at[j, p], d_r.at[j, p], "choice")
+        if k == 0:
+            for p in choice_peers:
+                arrived(kb.at[p], kv_r.at[0, p], "choice")
+                arrived(vb.at[p], kv_r.at[1, p], "choice")
+
+        def one(step, carry):
+            i = step // (rq // answer_rows)
+            inner = step % (rq // answer_rows)
+            q = sq_s[i, 0, j * (rq // answer_rows) + inner]
+            here = pl.ds(pl.multiple_of(step * answer_rows, answer_rows), answer_rows)
+            query = qr[j, 0, here, :].astype(jnp.float32)
+            for s in range(1, C):
+                query = query + qr[j, s, here, :].astype(jnp.float32)
+            query = query.astype(jnp.bfloat16)
+            zero = jnp.zeros_like(query)
+            stacked = jnp.concatenate(
+                [jnp.where(head_of_lane == h, query, zero) for h in range(heads)], axis=0
+            )
+            scores = lax.dot_general(
+                stacked, kb[q], (((1,), (1,)), ((), ())), preferred_element_type=jnp.float32
+            ) * scale
+            top = jnp.max(scores, axis=-1, keepdims=True)
+            e = jnp.exp(scores - top)
+            weights = (e * (1.0 / jnp.sum(e, axis=-1, keepdims=True))).astype(jnp.bfloat16)
+            mixed = jnp.dot(weights, vb[q], preferred_element_type=jnp.float32)
+            found = mixed[:answer_rows]
+            for h in range(1, heads):
+                found = jnp.where(head_of_lane == h, mixed[h * answer_rows : (h + 1) * answer_rows], found)
+            ctx[j, c, here, :] = found.astype(jnp.bfloat16)
+            return carry
+
+        lax.fori_loop(0, rows // answer_rows, one, 0)
+        for p in choice_peers:
+            send(ctx.at[j, c], ctx.at[j, c], e_s.at[j, p], e_r.at[j, c], "choice", p)
+
+    def mix(k):
+        j = flip(f, k)
+        for p in choice_peers:
+            arrived(ctx.at[j, p], e_r.at[j, p], "choice")
+        tile = hc
+        for t in range(kc // tile):
+            acc = jnp.dot(ctx[j, 0], wo[0:hc, t * tile : (t + 1) * tile], preferred_element_type=jnp.float32)
+            for s in range(1, C):
+                acc = acc + jnp.dot(
+                    ctx[j, s],
+                    wo[s * hc : (s + 1) * hc, t * tile : (t + 1) * tile],
+                    preferred_element_type=jnp.float32,
+                )
+            acc = acc.astype(jnp.bfloat16)
+            if k > 0:
+                osend[j, :, t * tile : (t + 1) * tile] = acc
+            else:
+                orecv[j, :, t * tile : (t + 1) * tile] = acc
+        if k > 0:
+            send(osend.at[j], orecv.at[f], g_s.at[j], g_r.at[f], "fsdp", j)
+
+    for k in range(F + 2):
+        if k < F:
+            project(k)
+        if 1 <= k <= F:
+            attend(k - 1)
+        if k >= 2:
+            mix(k - 2)
+
+    for p in fsdp_peers:
+        arrived(orecv.at[p], g_r.at[p], "fsdp")
+
+    def gathered(i):
+        here = pl.ds(pl.multiple_of(i * rq, rq), rq)
+        acc = orecv[0, here, :].astype(jnp.float32)
+        for s in range(1, F):
+            acc = acc + orecv[s, here, :].astype(jnp.float32)
+        return acc.astype(jnp.bfloat16)
+
+    for p in choice_peers:
+        asend[p] = gathered(p)
+        send(asend.at[p], arecv.at[c], h_s.at[p], h_r.at[c], "choice", p)
+    arecv[c] = gathered(c)
+
+    position = f * rq + lax.broadcasted_iota(jnp.int32, (rq, 1), 0)
+    slot = position // answer_rows
+    length = jnp.zeros((rq, 1), jnp.int32)
+    for s in range(lengths.shape[0]):
+        length = jnp.where(slot == s, lengths[s], length)
+    valid = position % answer_rows < length
+
+    def finish(i):
+        x = hrow[:, cols(i, kc)].astype(jnp.float32) + arecv[i].astype(jnp.float32)
+        out[:, cols(i, kc)] = jnp.where(valid, x, 0.0).astype(jnp.bfloat16)
+
+    finish(c)
+    for p in choice_peers:
+        arrived(arecv.at[p], h_r.at[p], "choice")
+        finish(p)
+    for copy in pending:
+        copy.wait_send()
+
+
+def in_one_kernel(
+    C, F, hidden, norm_gain, query_weight, out_weight, enc_keys, enc_values, slot_question, answer_len
+):
+    count = hidden.shape[0]
+    rq = count // F
+    df = hidden.shape[1]
+    D = df * F
+    kc, width = query_weight.shape
+    hc = width // C
+    rows = C * rq
+    enc = enc_keys.shape[1]
+    slots = slot_question.shape[0]
+    questions = jnp.pad(slot_question[None, :], ((0, 7), (0, 128 - slots)))
+    bf = jnp.bfloat16
+    vmem = pl.BlockSpec(memory_space=pltpu.VMEM)
+    dma = pltpu.SemaphoreType.DMA
+    return pl.pallas_call(
+        functools.partial(block_kernel, C, F, count // slots),
+        out_shape=jax.ShapeDtypeStruct((rq, D), bf),
+        in_specs=[vmem] * 7 + [pl.BlockSpec(memory_space=pltpu.SMEM)],
+        out_specs=vmem,
+        scratch_shapes=[
+            pltpu.VMEM((rq, D), bf),
+            pltpu.VMEM((C, rq, kc), bf),
+            pltpu.VMEM((F, C, rq, kc), bf),
+            pltpu.VMEM((F, C, rows, hc), bf),
+            pltpu.VMEM((F, C, rows, hc), bf),
+            pltpu.VMEM((C, enc, hc), bf),
+            pltpu.VMEM((C, enc, hc), bf),
+            pltpu.VMEM((C, 8, 128), jnp.int32),
+            pltpu.SMEM((C, 8, 128), jnp.int32),
+            pltpu.VMEM((F, C, rows, hc), bf),
+            pltpu.VMEM((F, rows, kc), bf),
+            pltpu.VMEM((F, rows, kc), bf),
+            pltpu.VMEM((C, rq, kc), bf),
+            pltpu.VMEM((C, rq, kc), bf),
+            dma((F,)),
+            dma((F,)),
+            dma((C,)),
+            dma((C,)),
+            dma((F, C)),
+            dma((F, C)),
+            dma((2, C)),
+            dma((2, C)),
+            dma((C,)),
+            dma((C,)),
+            dma((F, C)),
+            dma((F, C)),
+            dma((F, C)),
+            dma((F, C)),
+            dma((F,)),
+            dma((F,)),
+            dma((C,)),
+            dma((C,)),
+            dma,
+        ],
+        compiler_params=pltpu.CompilerParams(
+            collective_id=0, has_side_effects=True, vmem_limit_bytes=50 * 1024 * 1024
+        ),
+        cost_estimate=pl.CostEstimate(
+            flops=4 * F * rows * kc * width, bytes_accessed=8 * kc * width, transcendentals=F * rows * enc * (hc // HD)
+        ),
+    )(
+        hidden,
+        norm_gain.reshape(1, D),
+        query_weight,
+        out_weight,
+        enc_keys[0],
+        enc_values[0],
+        questions,
+        answer_len,
+    )
 
 
 def attend_rows(query_rows, keys_block, values_block):
@@ -26,6 +372,12 @@
     weights = jax.nn.softmax(scores, axis=-1).astype(jnp.bfloat16)
     context = jnp.einsum("hak,khd->ahd", weights, value_view, preferred_element_type=jnp.float32)
     return context.astype(jnp.bfloat16).reshape(count, width)
+
+
+def picked(choose, blocks):
+    return jnp.einsum(
+        "bs,sax->bax", choose.astype(jnp.bfloat16), blocks, preferred_element_type=jnp.float32
+    ).astype(jnp.bfloat16)
 
 
 def on_device(
@@ -54,9 +406,7 @@
     rank = jnp.sum(jnp.where(same_question & earlier, 1, 0), axis=1).astype(jnp.int32)
     target = slot_question * CAP + rank
     placed = jnp.arange(buffers, dtype=jnp.int32)[:, None] == target[None, :]
-    source_slot = jnp.sum(jnp.where(placed, slot_ids[None, :], 0), axis=1)
-    filled = jnp.any(placed, axis=1)
-    outgoing = jnp.where(filled[:, None, None], per_slot[source_slot], jnp.zeros((), jnp.bfloat16))
+    outgoing = picked(placed, per_slot)
     outgoing = outgoing.reshape(owners, CAP, answer_rows, columns)
     local_keys = enc_keys[0]
     local_values = enc_values[0]
@@ -69,7 +419,7 @@
         answer_source, lax.all_to_all(outgoing, "choice", split_axis=0, concat_axis=0, tiled=True)
     )
     returned = lax.all_to_all(answered, "choice", split_axis=0, concat_axis=0, tiled=True)
-    context = returned.reshape(buffers, answer_rows, columns)[target]
+    context = picked(placed.T, returned.reshape(buffers, answer_rows, columns))
     context_rows = context.reshape(total_rows, columns)
     out_full = lax.all_gather(out_weight, "choice", axis=1, tiled=True)
     share = total_rows // lax.axis_size("fsdp")
@@ -102,6 +452,24 @@
         P(("groups", "choice")),
     )
     out_specs = P(("groups", "choice", "fsdp"), None)
+    C = mesh.shape["choice"]
+    F = mesh.shape["fsdp"]
+
+    def body(*args):
+        hidden, query_weight, slot_question = args[0], args[2], args[6]
+        count = hidden.shape[0]
+        answer_rows = count // slot_question.shape[0]
+        fits = (
+            F & (F - 1) == 0
+            and count % F == 0
+            and (count // F) % answer_rows == 0
+            and query_weight.shape[1] % (C * 128) == 0
+            and query_weight.shape[0] % (query_weight.shape[1] // C) == 0
+            and F > 1
+            and C > 1
+        )
+        return in_one_kernel(C, F, *args) if fits else on_device(*args)
+
     return jax.shard_map(
-        on_device, mesh=mesh, in_specs=in_specs, out_specs=out_specs, check_vma=False
-    )
+        body, mesh=mesh, in_specs=in_specs, out_specs=out_specs, check_vma=False
+    )

time: 426 us -> 177 us (0.42)
  waiting for transfers between devices: 328 us -> 0 us
  Pallas kernels: 0 us -> 170 us
  matrix products: 41 us -> 0 us
  starting transfers between devices: 15.7 us -> 0 us
  between operations: 13.2 us -> 0.01 us
  local copies, waits for them, and re-layouts: 16.5 us -> 5.95 us
  other arithmetic: 8.61 us -> 0 us
    all_gather x3 -> x0, waiting for transfers between devices: 202 us -> none  [the longest x1 147 us: on_device(): lax.all_gather(query_weight, 'choice', axis=0, tiled=True)]
    pallas_call x0 -> x1, Pallas kernels: none -> 170 us  [in_one_kernel(): pl.pallas_call(functools.partial(block_kernel, C, F, count // slots), out...]
    all_to_all x2 -> x0, waiting for transfers between devices: 93.9 us -> none  [the longest x1 49.3 us: on_device(): lax.all_to_all(answered, 'choice', split_axis=0, concat_axis=0, tiled=True)]
    dot_general x6 -> x0, matrix products: 32.9 us -> none  [the longest x4 19 us: attend_rows(): jnp.einsum('hak,khd->ahd', weights, value_view, preferred_element_type=jn...]
    reduce_scatter x1 -> x0, waiting for transfers between devices: 29.4 us -> none  [on_device(): lax.psum_scatter(jnp.dot(section, out_full, preferred_element_type=jnp.fl...]
    all_to_all x2 -> x0, starting transfers between devices: 15.6 us -> none  [the longest x1 7.93 us: on_device(): lax.all_to_all(answered, 'choice', split_axis=0, concat_axis=0, tiled=True)]
    sub x4 -> x0, matrix products: 8.14 us -> none  [attend_rows(): weights = jax.nn.softmax(scores, axis=-1).astype(jnp.bfloat16)]
    convert_element_type x2 -> x0, other arithmetic: 4.75 us -> none  [the longest x1 2.42 us: on_device(): widened = whole.astype(jnp.float32)]
  transfers between devices with their start and end apart: 6 -> 0, of which waited for: 6 -> 0; matrix products, arithmetic and copies ran while one was open for 13% -> 0% of each run, Pallas kernels for 0% -> 0%
where the time goes in v1:
time: 177 us; the launch traced here: 176 us
  Pallas kernels  170 us (96%)
  local copies, waits for them, and re-layouts  5.95 us (3%)
    pallas_call x1, Pallas kernels, in_one_kernel(): pl.pallas_call(functools.partial(block_kernel, C, F, count // slots), out...  170 us
    unnamed x11, local copies, waits for them, and re-layouts  5.29 us

profile of v1, /device:TPU:15, one launch (start us, length us, event | category | flops | bytes accessed | tf_op | source)
XLA Modules:
  0.0 176.2 jit_solution(12455796166782819780)
XLA Ops:
  0.0 0.7 pad.4.questions
  0.7 0.0 copy-start
  0.7 1.0 copy-done
  1.7 0.0 copy-start.1
  1.7 1.0 copy-done.1
  2.7 0.0 copy-start.2
  2.7 1.0 copy-done.2
  3.8 0.0 copy-start.3
  3.8 0.7 copy-done.3
  4.5 0.0 copy-start.4
  4.5 0.7 copy-done.4
  5.2 170.3 %shard_map.82 = bf16[64,4096]{1,0:T(8,128)(2,1)S(1)} custom-call(bf16[256,1024]{1,0:T(8,128)(2,1)S(1)} %copy-done, f32[1,4096]{1,0:T(1,128)S(1)} %bitcast.6, bf16[1024,1024]{1,0:T(8,128)(2,1)} %wq.1, bf16[1024,1024]{1,0:T(8,128)(2,1)} %wo.1, bf16[256,1024]{1,0:T(8,128)(2,1)S(1)} %bitcast.4, bf16[256,1024]{1,0:T(8,128)(2,1)S(1)} %bitcast.5, ...), custom_call_target="tpu_custom_call" | custom-call | flops 4294967296 | bytes 8388608 | tf_op jit(solution)/shard_map/pallas_call | solution.py:303
  175.4 0.8 copy.10
Async XLA Ops:
  0.7 1.0 copy-start
  1.7 1.0 copy-start.1
  2.7 1.0 copy-start.2
  3.8 0.7 copy-start.3
  4.5 0.7 copy-start.4

commit v2 on v1

--- a/solution.py
+++ b/solution.py
@@ -42,14 +42,16 @@
     answer_rows,
     hidden,
     gain,
-    wq,
-    wo,
+    wq_hbm,
+    wo_hbm,
     keys,
     values,
     questions,
     lengths,
     out,
     hrow,
+    wq,
+    wo,
     xs,
     xn,
     qs,
@@ -123,7 +125,19 @@
 
     for p in fsdp_peers:
         send(hidden.at[part(p)], hrow.at[:, cols(f, df)], a_s.at[p], a_r.at[f], "fsdp", p)
-    hrow[:, cols(f, df)] = hidden[part(f), :]
+    def bring(src, dst, i):
+        copy = pltpu.make_async_copy(src, dst, local.at[i])
+        copy.start()
+        return copy
+
+    own_rows = bring(hidden.at[part(f)], hrow.at[:, cols(f, df)], 0)
+    own_keys = bring(keys.at[:, cols(c, hc)], kb.at[c], 1)
+    query_copy = bring(wq_hbm, wq, 2)
+    own_values = bring(values.at[:, cols(c, hc)], vb.at[c], 3)
+    out_copy = bring(wo_hbm, wo, 4)
+    for p in choice_peers:
+        send(keys.at[:, cols(p, hc)], kb.at[c], kv_s.at[0, p], kv_r.at[0, c], "choice", p)
+    own_rows.wait()
     for p in fsdp_peers:
         arrived(hrow.at[:, cols(p, df)], a_r.at[p], "fsdp")
 
@@ -152,17 +166,16 @@
             send(xn.at[f, p], xn.at[f, p], c_s.at[o, p], c_r.at[f, p], "fsdp", o)
 
     for p in choice_peers:
-        send(keys.at[:, cols(p, hc)], kb.at[c], kv_s.at[0, p], kv_r.at[0, c], "choice", p)
         send(values.at[:, cols(p, hc)], vb.at[c], kv_s.at[1, p], kv_r.at[1, c], "choice", p)
-    kb[c] = keys[:, cols(c, hc)]
-    vb[c] = values[:, cols(c, hc)]
     sq[c] = questions[...]
 
     head_of_lane = lax.broadcasted_iota(jnp.int32, (1, hc), 1) // HD
 
     def project(k):
         j = flip(f, k)
-        if k > 0:
+        if k == 0:
+            query_copy.wait()
+        else:
             for i in range(C):
                 arrived(xn.at[j, i], c_r.at[j, i], "fsdp")
         for t in range(1, C + 1):
@@ -181,12 +194,14 @@
         if k == 0:
             for p in choice_peers:
                 arrived(sq.at[p], sq_r.at[p], "choice")
-            copy = pltpu.make_async_copy(sq, sq_s, local)
+            copy = pltpu.make_async_copy(sq, sq_s, local.at[5])
             copy.start()
             copy.wait()
         for p in choice_peers:
             arrived(qr.at[j, p], d_r.at[j, p], "choice")
         if k == 0:
+            own_keys.wait()
+            own_values.wait()
             for p in choice_peers:
                 arrived(kb.at[p], kv_r.at[0, p], "choice")
                 arrived(vb.at[p], kv_r.at[1, p], "choice")
@@ -218,13 +233,48 @@
             return carry
 
         lax.fori_loop(0, rows // answer_rows, one, 0)
-        for p in choice_peers:
-            send(ctx.at[j, c], ctx.at[j, c], e_s.at[j, p], e_r.at[j, c], "choice", p)
+        pass_on(j, c, 1)
+        pass_on(j, c, -1)
+
+    def has(step):
+        return c < C - 1 if step > 0 else c > 0
+
+    def hop(j, s, step):
+        return remote(
+            ctx.at[j, s], ctx.at[j, s], e_s.at[(step + 1) // 2, j, s], e_r.at[j, s], "choice", lax.rem(c + step + C, C)
+        )
+
+    def pass_on(j, s, step):
+        @pl.when(has(step))
+        def _():
+            hop(j, s, step).start()
+
+    def relay(k):
+        j = flip(f, k)
+        for t in range(1, C):
+            for step in (1, -1):
+                s = c - t * step
+
+                @pl.when((s >= 0) & (s < C))
+                def _():
+                    arrived(ctx.at[j, s], e_r.at[j, s], "choice")
+                    pass_on(j, s, step)
+
+    def settle(k):
+        j = flip(f, k)
+        for t in range(C):
+            for step in (1, -1):
+                s = c - t * step
+
+                @pl.when((s >= 0) & (s < C) & has(step))
+                def _():
+                    hop(j, s, step).wait_send()
 
     def mix(k):
         j = flip(f, k)
-        for p in choice_peers:
-            arrived(ctx.at[j, p], e_r.at[j, p], "choice")
+        relay(k)
+        if k == 0:
+            out_copy.wait()
         tile = hc
         for t in range(kc // tile):
             acc = jnp.dot(ctx[j, 0], wo[0:hc, t * tile : (t + 1) * tile], preferred_element_type=jnp.float32)
@@ -240,21 +290,22 @@
             else:
                 orecv[j, :, t * tile : (t + 1) * tile] = acc
         if k > 0:
-            send(osend.at[j], orecv.at[f], g_s.at[j], g_r.at[f], "fsdp", j)
-
+            for i in choice_peers + [c]:
+                send(osend.at[j, part(i)], orecv.at[f, part(i)], g_s.at[j, i], g_r.at[f, i], "fsdp", j)
+
+    order = [0] + list(range(2, F)) + [1]
     for k in range(F + 2):
         if k < F:
-            project(k)
+            project(order[k])
         if 1 <= k <= F:
-            attend(k - 1)
+            attend(order[k - 1])
         if k >= 2:
-            mix(k - 2)
-
-    for p in fsdp_peers:
-        arrived(orecv.at[p], g_r.at[p], "fsdp")
+            mix(order[k - 2])
 
     def gathered(i):
-        here = pl.ds(pl.multiple_of(i * rq, rq), rq)
+        here = part(i)
+        for p in fsdp_peers:
+            arrived(orecv.at[p, here], g_r.at[p, i], "fsdp")
         acc = orecv[0, here, :].astype(jnp.float32)
         for s in range(1, F):
             acc = acc + orecv[s, here, :].astype(jnp.float32)
@@ -282,6 +333,8 @@
         finish(p)
     for copy in pending:
         copy.wait_send()
+    for k in range(F):
+        settle(k)
 
 
 def in_one_kernel(
@@ -299,14 +352,17 @@
     questions = jnp.pad(slot_question[None, :], ((0, 7), (0, 128 - slots)))
     bf = jnp.bfloat16
     vmem = pl.BlockSpec(memory_space=pltpu.VMEM)
+    hbm = pl.BlockSpec(memory_space=pl.ANY)
     dma = pltpu.SemaphoreType.DMA
     return pl.pallas_call(
         functools.partial(block_kernel, C, F, count // slots),
         out_shape=jax.ShapeDtypeStruct((rq, D), bf),
-        in_specs=[vmem] * 7 + [pl.BlockSpec(memory_space=pltpu.SMEM)],
+        in_specs=[hbm, vmem, hbm, hbm, hbm, hbm, vmem] + [pl.BlockSpec(memory_space=pltpu.SMEM)],
         out_specs=vmem,
         scratch_shapes=[
             pltpu.VMEM((rq, D), bf),
+            pltpu.VMEM((kc, width), bf),
+            pltpu.VMEM((width, kc), bf),
             pltpu.VMEM((C, rq, kc), bf),
             pltpu.VMEM((F, C, rq, kc), bf),
             pltpu.VMEM((F, C, rows, hc), bf),
@@ -332,13 +388,13 @@
             dma((C,)),
             dma((F, C)),
             dma((F, C)),
-            dma((F, C)),
-            dma((F, C)),
-            dma((F,)),
-            dma((F,)),
+            dma((2, F, C)),
+            dma((F, C)),
+            dma((F, C)),
+            dma((F, C)),
             dma((C,)),
             dma((C,)),
-            dma,
+            dma((6,)),
         ],
         compiler_params=pltpu.CompilerParams(
             collective_id=0, has_side_effects=True, vmem_limit_bytes=50 * 1024 * 1024

time: 177 us -> 142 us (0.80)
  Pallas kernels: 170 us -> 135 us
    pallas_call x1, Pallas kernels: 170 us -> 135 us  [in_one_kernel(): pl.pallas_call(functools.partial(block_kernel, C, F, count // slots), out...]
where the time goes in v2:
time: 142 us; the launch traced here: 141 us
  Pallas kernels  135 us (95%)
  local copies, waits for them, and re-layouts  5.95 us (4%)
    pallas_call x1, Pallas kernels, in_one_kernel(): pl.pallas_call(functools.partial(block_kernel, C, F, count // slots), out...  135 us
    unnamed x11, local copies, waits for them, and re-layouts  5.29 us

profile of v2, /device:TPU:15, one launch (start us, length us, event | category | flops | bytes accessed | tf_op | source)
XLA Modules:
  0.0 140.5 jit_solution(3600794367018254310)
XLA Ops:
  0.0 0.7 pad.4.questions
  0.7 0.0 copy-start
  0.7 1.0 copy-done
  1.7 0.0 copy-start.1
  1.7 1.0 copy-done.1
  2.7 0.0 copy-start.2
  2.7 1.0 copy-done.2
  3.8 0.0 copy-start.3
  3.8 0.7 copy-done.3
  4.5 0.0 copy-start.4
  4.5 0.7 copy-done.4
  5.2 134.6 %shard_map.82 = bf16[64,4096]{1,0:T(8,128)(2,1)S(1)} custom-call(bf16[256,1024]{1,0:T(8,128)(2,1)S(1)} %copy-done, f32[1,4096]{1,0:T(1,128)S(1)} %bitcast.6, bf16[1024,1024]{1,0:T(8,128)(2,1)} %wq_hbm.1, bf16[1024,1024]{1,0:T(8,128)(2,1)} %wo_hbm.1, bf16[256,1024]{1,0:T(8,128)(2,1)S(1)} %bitcast.4, bf16[256,1024]{1,0:T(8,128)(2,1)S(1)} %bitcast.5, ...), custom_call_target="tpu_custom_call" | custom-call | flops 4294967296 | bytes 8388608 | tf_op jit(solution)/shard_map/pallas_call | solution.py:357
  139.7 0.8 copy.10
Async XLA Ops:
  0.7 1.0 copy-start
  1.7 1.0 copy-start.1
  2.7 1.0 copy-start.2
  3.8 0.7 copy-start.3
  4.5 0.7 copy-start.4
